TPU v7x, 32 devices: a whole 2x2x4 slice. The times are simulated.
32 devices in a mesh: groups: 2 (over y), dp: 4 (over z), split: 4 (over x, core).
Axes of the slice: x: 2, y: 2, z: 4, core: 2. Of those that a mesh axis runs over, the one named last changes fastest.
Arguments:
- embeddings: bfloat16 [32768, 1536], P(('groups', 'dp', 'split')), parts along dimension 0, may hold values from -144 to 144
- subcentroids: bfloat16 [8, 256, 1536], P(('groups', 'dp')), parts along dimension 0, may hold values from -16 to 16
- block_cluster: int32 [256], P(('groups', 'dp', 'split')), parts along dimension 0, may hold values from 0 to 3, as said below
- owner_map: int32 [8], P('groups'), parts along dimension 0, may hold values from 0 to 3, each once
Outputs:
- assignment: bfloat16 [32768, 256], P(('groups', 'dp', 'split')), parts along dimension 0
- centres: bfloat16 [8, 256, 1536], P(('groups', 'dp'), 'split'), parts along dimension 0
There are 2 independent parts, one for each index of `groups`. A program takes and returns all parts, laid end to end along the dimension named above; each array names one. Nothing has to cross between parts.
Inputs may be any that keep to these rules, and one draw needn't show every extreme that they name: `block_cluster`: among the 8 blocks of one device no cluster is named more than 4 times; one cluster, the same for every device, is named exactly 4 times by every device. `owner_map`: A permutation.
All inputs are finite; a program needn't handle non-finite values.
Results may differ from a plain program's by a relative error of at most 0.008.
Values may be sent and summed in bfloat16 or wider, within the bound.
A program may use at most 128 MiB of HBM per device.

v0:
```python
import jax
import jax.numpy as jnp
from jax import lax
from jax.sharding import PartitionSpec as P

ITERS = 2


prior_mass = 4.0


def soft_weights(flat_rows, centre):
    inv_root = flat_rows.shape[1] ** (-0.5)
    dots = lax.dot_general(
        flat_rows, centre, (((1,), (1,)), ((), ())), preferred_element_type=jnp.float32
    )
    squares = jnp.sum(jnp.square(centre.astype(jnp.float32)), axis=1)
    logits = (2.0 * dots - squares[None, :]) * inv_root
    return jax.nn.softmax(logits, axis=-1).astype(jnp.bfloat16)


def renew(weighted, weight_mass, previous):
    return (
        (weighted + prior_mass * previous.astype(jnp.float32))
        / (weight_mass[..., None] + prior_mass)
    ).astype(jnp.bfloat16)


def body(embeddings, subcentroids, block_cluster, owner_map):
    dp_count = lax.axis_size("dp")
    split_count = lax.axis_size("split")
    block_count = block_cluster.shape[0]
    row_total = embeddings.shape[0]
    feature_count = embeddings.shape[1]
    block_rows = row_total // block_count
    capacity = max(2, 2 * block_count // dp_count)
    slot_count = dp_count * capacity
    sub_count = subcentroids.shape[1]
    current = subcentroids[0]
    cluster_ids = jnp.arange(dp_count, dtype=jnp.int32)
    owner_dev = jnp.sum(
        jnp.where(block_cluster[:, None] == cluster_ids[None, :], owner_map[None, :], 0), axis=1
    )
    block_ids = jnp.arange(block_count, dtype=jnp.int32)
    earlier = (owner_dev[:, None] == owner_dev[None, :]) & (block_ids[None, :] < block_ids[:, None])
    slot_of = owner_dev * capacity + jnp.sum(earlier.astype(jnp.int32), axis=1)
    matches = slot_of[None, :] == jnp.arange(slot_count, dtype=jnp.int32)[:, None]
    source_block = jnp.sum(jnp.where(matches, block_ids[None, :], 0), axis=1)
    occupied = jnp.any(matches, axis=1)
    blocks = embeddings.reshape(block_count, block_rows, feature_count)
    outgoing = jnp.where(
        occupied[:, None, None], jnp.take(blocks, source_block, axis=0), jnp.zeros((), jnp.bfloat16)
    )
    outgoing = outgoing.reshape(dp_count, capacity, block_rows, feature_count)
    flags = occupied.astype(jnp.bfloat16).reshape(dp_count, capacity)
    first_scores = None
    incoming, present = (
        lax.all_to_all(outgoing, "dp", split_axis=0, concat_axis=0, tiled=True),
        lax.all_to_all(flags, "dp", split_axis=0, concat_axis=0, tiled=True),
    )
    flat_rows = incoming.reshape(-1, feature_count)
    live_rows = jnp.broadcast_to(present[:, :, None], present.shape + (block_rows,)).reshape(-1) > 0
    portion = sub_count // split_count
    offset = lax.axis_index("split") * portion
    weights = None
    owned = None
    for sweep in range(ITERS):
        weights = soft_weights(flat_rows, current)
        masked = jnp.where(live_rows[:, None], weights, jnp.zeros((), jnp.bfloat16))
        weighted = lax.dot_general(
            masked, flat_rows, (((0,), (0,)), ((), ())), preferred_element_type=jnp.float32
        )
        weight_mass = jnp.sum(masked, axis=0, dtype=jnp.float32)
        summed, mass_all = lax.psum((weighted, weight_mass), "split")
        current = renew(summed, mass_all, current)
        owned = lax.dynamic_slice_in_dim(current, offset, portion, 0)
    outward = weights.reshape(dp_count, capacity, block_rows, sub_count)
    returned = lax.all_to_all(outward, "dp", split_axis=0, concat_axis=0, tiled=True)
    at_home = jnp.take(returned.reshape(slot_count, block_rows, sub_count), slot_of, axis=0)
    return (at_home.reshape(row_total, sub_count), owned[None])


def solution(mesh):
    return jax.shard_map(
        body,
        mesh=mesh,
        in_specs=(
            P(("groups", "dp", "split"), None),
            P(("groups", "dp"), None, None),
            P(("groups", "dp", "split")),
            P("groups"),
        ),
        out_specs=(P(("groups", "dp", "split"), None), P(("groups", "dp"), "split", None)),
        check_vma=False,
    )
```

profile of v0, /device:TPU:0, one launch (start us, length us, event | category | flops | bytes accessed | tf_op | source)
XLA Modules:
  0.0 307.5 jit_solution(13250357723161206504)
XLA Ops:
  7.2 0.9 select_reduce_fusion.1
  9.0 6.3 %all-to-all-start.1 = ((bf16[4,1,4]{2,1,0:T(2,128)(2,1)}), bf16[4,1,4]{2,1,0:T(2,128)(2,1)S(1)}, u32[]{:S(2)}, u32[]{:S(2)}) async-start(bf16[4,1,4]{2,1,0:T(2,128)(2,1)} %reshape.145), calls=%async_computation.1 | async-start | bytes 4096 | tf_op jit(solution)/shard_map/all_to_all | solution.py:59
  15.7 3.6 %gather_fusion = bf16[16,128,1536]{2,1,0:T(8,128)(2,1)} fusion(bf16[8,128,1536]{2,1,0:T(8,128)(2,1)S(1)} %bitcast.38, s32[1024]{0:T(1024)S(1)} %pad_clamp_fusion.1), kind=kCustom, calls=%fused_computation | custom fusion | bytes 12582976 | tf_op jit(solution)/shard_map/jit(_take)/gather | solution.py:52
  19.3 6.2 %select_select_fusion = bf16[4,4,128,1536]{3,2,1,0:T(8,128)(2,1)} fusion(bf16[4,4,128,1536]{3,2,1,0:T(8,128)(2,1)} %bitcast.39, pred[4,4]{1,0:T(4,128)(4,1)S(1)} %compare_and_fusion, pred[4,4]{1,0:T(4,128)(4,1)S(1)} %broadcast_in_dim.113), kind=kLoop, calls=%fused_computation.2 | loop fusion | flops 6291456 | bytes 12582944 | tf_op jit(solution)/shard_map/jit(_where)/select_n | solution.py:51
  25.5 5.2 %all-to-all-start = ((bf16[4,4,128,1536]{3,2,1,0:T(8,128)(2,1)}), bf16[4,4,128,1536]{3,2,1,0:T(8,128)(2,1)}, u32[]{:S(2)}, u32[]{:S(2)}) async-start(bf16[4,4,128,1536]{3,2,1,0:T(8,128)(2,1)} %select_select_fusion), calls=%async_computation | async-start | bytes 12582912 | tf_op jit(solution)/shard_map/all_to_all | solution.py:58
  30.8 1.4 fusion.6
  32.2 136.7 %all-to-all-done = bf16[4,4,128,1536]{3,2,1,0:T(8,128)(2,1)} async-done(((bf16[4,4,128,1536]{3,2,1,0:T(8,128)(2,1)}), bf16[4,4,128,1536]{3,2,1,0:T(8,128)(2,1)}, u32[]{:S(2)}, u32[]{:S(2)}) %all-to-all-start) | async-done | bytes 6291488 | tf_op jit(solution)/shard_map/all_to_all | solution.py:58
  168.8 4.8 %fusion.25 = (f32[2048]{0:T(1024)S(1)}, f32[2048,256]{0,1:T(8,128)S(1)}) fusion(f32[256]{0:T(256)S(1)} %fusion.6, bf16[2048,1536]{1,0:T(8,128)(2,1)} %bitcast.5, bf16[1,256,1536]{2,1,0:T(8,128)(2,1)} %param.5), kind=kOutput, calls=%fused_computation.61 | convolution fusion | flops 1612707840 | bytes 9184256 | tf_op jit(solution)/shard_map/dot_general | solution.py:14
  174.6 5.7 %fusion.27 = f32[256,1536]{1,0:T(8,128)} fusion(bf16[2048,256]{0,1:T(8,128)(2,1)S(1)} %get-tuple-element.9, bf16[2048,1536]{1,0:T(8,128)(2,1)} %bitcast.5), kind=kOutput, calls=%fused_computation.63 | convolution fusion | flops 1610612736 | bytes 8912896 | tf_op jit(solution)/shard_map/dot_general | solution.py:70
  180.4 5.8 %psum.29 = f32[256]{0:T(256)S(1)} all-reduce(f32[256]{0:T(256)S(1)} %get-tuple-element.8), channel_id=1, replica_groups=mesh['groups'=2,'dp'=4,'split'=4] {'split'}, use_global_device_ids=true, to_apply=%region_9.10 | all-reduce | flops 256 | bytes 2048 | tf_op jit(solution)/shard_map/psum | solution.py:74
  186.2 36.3 %all-reduce.3.cloned.1.call-done = f32[256,1536]{1,0:T(8,128)} async-done(((f32[256,1536]{1,0:T(8,128)}), f32[256,1536]{1,0:T(8,128)}) %all-reduce.3.cloned.1.call-update) | async-done | bytes 1572880 | tf_op jit(solution)/shard_map/psum | solution.py:74
  222.5 3.1 %fusion.22 = (f32[256,1536]{1,0:T(8,128)}, bf16[256,1536]{1,0:T(8,128)(2,1)S(1)}) fusion(f32[256]{0:T(256)S(1)} %broadcast_add_fusion.1, f32[256,1536]{1,0:T(8,128)} %all-reduce.3.cloned.1.call-done, bf16[1,256,1536]{2,1,0:T(8,128)(2,1)} %param.5), kind=kLoop, calls=%fused_computation.60 | loop fusion | flops 2359296 | bytes 4719616 | tf_op jit(solution)/shard_map/convert_element_type | solution.py:17
  225.8 4.6 %fusion.26 = (f32[2048]{0:T(1024)S(1)}, f32[2048,256]{0,1:T(8,128)S(1)}) fusion(f32[256]{0:T(256)S(1)} %multiply_reduce_fusion, bf16[2048,1536]{1,0:T(8,128)(2,1)} %bitcast.5, bf16[256,1536]{1,0:T(8,128)(2,1)S(1)} %get-tuple-element.3), kind=kOutput, calls=%fused_computation.62 | convolution fusion | flops 1612707840 | bytes 9184256 | tf_op jit(solution)/shard_map/dot_general | solution.py:14
  230.7 1.5 convert_reduce_fusion
  232.3 2.6 reshape.126
  234.9 2.6 copy.19
  237.5 4.6 %all-to-all-start.2 = ((bf16[4,4,128,256]{2,1,3,0:T(4,128)(2,1)}), bf16[4,4,128,256]{2,1,3,0:T(4,128)(2,1)}, u32[]{:S(2)}, u32[]{:S(2)}) async-start(bf16[4,4,128,256]{2,1,3,0:T(4,128)(2,1)} %copy.19), calls=%async_computation.2 | async-start | bytes 2097152 | tf_op jit(solution)/shard_map/all_to_all | solution.py:78
  242.1 6.1 %fusion.11 = f32[256,1536]{1,0:T(8,128)} fusion(bf16[2048,1536]{1,0:T(8,128)(2,1)} %bitcast.5, bf16[2048,256]{0,1:T(8,128)(2,1)} %get-tuple-element.5, pred[2048]{0:T(1024)(128)(4,1)S(1)} %bitcast.43), kind=kOutput, calls=%fused_computation.26 | convolution fusion | flops 1611137024 | bytes 8914944 | tf_op jit(solution)/shard_map/dot_general | solution.py:70
  248.3 6.0 %psum.31 = f32[256]{0:T(256)S(1)} all-reduce(f32[256]{0:T(256)S(1)} %get-tuple-element.4), channel_id=1, replica_groups=mesh['groups'=2,'dp'=4,'split'=4] {'split'}, use_global_device_ids=true, to_apply=%region_15.16 | all-reduce | flops 256 | bytes 2048 | tf_op jit(solution)/shard_map/psum | solution.py:74
  254.4 37.3 %all-reduce.5.cloned.1.call-done = f32[256,1536]{1,0:T(8,128)} async-done(((f32[256,1536]{1,0:T(8,128)}), f32[256,1536]{1,0:T(8,128)}) %all-reduce.5.cloned.1.call-update) | async-done | bytes 1572880 | tf_op jit(solution)/shard_map/psum | solution.py:74
  291.8 1.9 fusion.16
  293.7 2.3 copy.20
  296.0 2.6 gather_fusion.1
  298.6 2.0 bitcast_select_fusion
  (32 shorter events, 3.0 us)
Async XLA Ops:
  7.2 8.5 %copy-start = (bf16[1024,1536]{1,0:T(8,128)(2,1)S(1)}, bf16[1024,1536]{1,0:T(8,128)(2,1)}, u32[]{:S(2)}) copy-start(bf16[1024,1536]{1,0:T(8,128)(2,1)} %param.4) | copy-start | bytes 9437188
  9.0 16.4 %all-to-all-start.1 = ((bf16[4,1,4]{2,1,0:T(2,128)(2,1)}), bf16[4,1,4]{2,1,0:T(2,128)(2,1)S(1)}, u32[]{:S(2)}, u32[]{:S(2)}) async-start(bf16[4,1,4]{2,1,0:T(2,128)(2,1)} %reshape.145), calls=%async_computation.1 | async-start | bytes 4096 | tf_op jit(solution)/shard_map/all_to_all | solution.py:59
  25.5 143.4 %all-to-all-start = ((bf16[4,4,128,1536]{3,2,1,0:T(8,128)(2,1)}), bf16[4,4,128,1536]{3,2,1,0:T(8,128)(2,1)}, u32[]{:S(2)}, u32[]{:S(2)}) async-start(bf16[4,4,128,1536]{3,2,1,0:T(8,128)(2,1)} %select_select_fusion), calls=%async_computation | async-start | bytes 12582912 | tf_op jit(solution)/shard_map/all_to_all | solution.py:58
  30.7 191.8 %all-reduce.3.cloned.1.call-start = ((), (), s32[]{:S(2)}) async-start(), calls=%async_computation.3 | async-start | bytes 3145728 | tf_op jit(solution)/shard_map/psum | solution.py:74
  237.5 56.2 %all-to-all-start.2 = ((bf16[4,4,128,256]{2,1,3,0:T(4,128)(2,1)}), bf16[4,4,128,256]{2,1,3,0:T(4,128)(2,1)}, u32[]{:S(2)}, u32[]{:S(2)}) async-start(bf16[4,4,128,256]{2,1,3,0:T(4,128)(2,1)} %copy.19), calls=%async_computation.2 | async-start | bytes 2097152 | tf_op jit(solution)/shard_map/all_to_all | solution.py:78
  242.1 49.7 %all-reduce.5.cloned.1.call-start = ((), (), s32[]{:S(2)}) async-start(), calls=%async_computation.4 | async-start | bytes 3145728 | tf_op jit(solution)/shard_map/psum | solution.py:74
Sparse Core Ops, SparseCore 0:
  180.5 41.9 all-reduce.2
  248.3 43.3 all-reduce.4
where the time goes:
time: 308 us; the launch traced here: 307 us
  waiting for transfers between devices  210 us (68%)
  matrix products  21.3 us (7%)
  other arithmetic  18.9 us (6%)
  starting transfers between devices  16.2 us (5%)
  local copies, waits for them, and re-layouts  14.8 us (5%)
  between operations  14.1 us (5%)
  blocking collectives  11.8 us (4%)
    all_to_all x1, waiting for transfers between devices, body(): lax.all_to_all(outgoing, 'dp', split_axis=0, concat_axis=0, tiled=True)  137 us
    psum x2, waiting for transfers between devices, body(): summed, mass_all = lax.psum((weighted, weight_mass), 'split')  73.7 us
    dot_general x2, matrix products, body(): lax.dot_general(masked, flat_rows, (((0,), (0,)), ((), ())), preferred_el...  11.9 us
    psum x2, blocking collectives, body(): summed, mass_all = lax.psum((weighted, weight_mass), 'split')  11.8 us
    dot_general x2, matrix products, soft_weights(): lax.dot_general(flat_rows, centre, (((1,), (1,)), ((), ())), preferred_el...  9.41 us
    all_to_all x1, starting transfers between devices, body(): lax.all_to_all(flags, 'dp', split_axis=0, concat_axis=0, tiled=True)  6.32 us
    select_n x1, other arithmetic, body(): jnp.where(occupied[:, None, None], jnp.take(blocks, source_block, axis=0)...  6.19 us
  transfers between devices with their start and end apart: 5, of which 3 were waited for; matrix products, arithmetic and copies ran while one was open for 6% of the time, Pallas kernels for 0%

commit v1 on v0

v1 whole, which is shorter than its diff:
```python
import functools

import jax
import jax.numpy as jnp
from jax import lax
from jax.experimental import pallas as pl
from jax.experimental.pallas import tpu as pltpu
from jax.sharding import PartitionSpec as P

MESH = pl.DeviceIdType.MESH
ITERS = 2
PRIOR = 4.0
LANES = 128


def split_mass(mass):
    high = mass.astype(jnp.bfloat16).astype(jnp.float32)
    lane = lax.broadcasted_iota(jnp.int32, (mass.shape[0], LANES), 1)
    return jnp.where(lane < LANES // 2, high, mass - high).astype(jnp.bfloat16)


def join_mass(pair):
    return pair[:, :1] + pair[:, LANES // 2 : LANES // 2 + 1]


def kernel(
    owners, chips, cap,
    cluster_ref, owner_ref, rows_hbm, sub_hbm,
    weight_out, centre_out,
    rows, cents, wts, squares, wcat, part, from_core, from_chip, from_owner,
    load_sem, gz_send, gz_recv, gx_send, gx_recv, gc_send, gc_recv,
    rc_send, rc_recv, rx_send, rx_recv, rz_send, rz_recv,
):
    blocks, block_rows, width = rows.shape
    parts, portion = cents.shape[1], cents.shape[2]
    subs = parts * portion
    inv_root = width ** (-0.5)
    z = lax.axis_index("dp")
    s = lax.axis_index("split")
    x = lax.div(s, 2)
    c = s - 2 * x
    sibling = 2 * x + (1 - c)

    def owner_at(i):
        return lax.rem(z + i, owners)

    def chip_at(j):
        return lax.rem(x + j, chips)

    def remote(src, dst, send, recv, axis, index):
        return pltpu.make_async_remote_copy(
            src_ref=src, dst_ref=dst, send_sem=send, recv_sem=recv,
            device_id={axis: index}, device_id_type=MESH,
        )

    load_rows = pltpu.make_async_copy(rows_hbm, rows, load_sem.at[0])
    load_sub = pltpu.make_async_copy(sub_hbm, cents.at[z], load_sem.at[1])
    load_sub.start()
    load_rows.start()

    barrier = pltpu.get_barrier_semaphore()
    pl.semaphore_signal(barrier, inc=1, device_id={"split": sibling}, device_id_type=MESH)
    for j in range(1, chips):
        pl.semaphore_signal(barrier, inc=1, device_id={"split": 2 * chip_at(j) + c}, device_id_type=MESH)
    for i in range(1, owners):
        pl.semaphore_signal(barrier, inc=1, device_id={"dp": owner_at(i)}, device_id_type=MESH)
    pl.semaphore_wait(barrier, 1 + (chips - 1) + (owners - 1))
    load_sub.wait()

    def gz(i):
        ref = cents.at[z, s]
        return remote(ref, ref, gz_send.at[i], gz_recv.at[z], "dp", lax.rem(z + owners - i, owners))

    def gz_from(o):
        ref = cents.at[o, s]
        return remote(ref, ref, gz_send.at[0], gz_recv.at[o], "dp", owner_at(1))

    def gx(o, j):
        ref = cents.at[o, s]
        return remote(ref, ref, gx_send.at[o, j], gx_recv.at[o, x], "split", 2 * chip_at(j) + c)

    def gx_from(o, j):
        ref = cents.at[o, 2 * chip_at(j) + c]
        return remote(ref, ref, gx_send.at[o, j], gx_recv.at[o, chip_at(j)], "split", 2 * chip_at(j) + c)

    def gc(o, chip):
        ref = cents.at[o, 2 * chip + c]
        return remote(ref, ref, gc_send.at[o, chip], gc_recv.at[o, chip], "split", sibling)

    def gc_from(o, chip):
        ref = cents.at[o, 2 * chip + 1 - c]
        return remote(ref, ref, gc_send.at[o, chip], gc_recv.at[o, chip], "split", sibling)

    def gather(first):
        for i in range(1, owners):
            gz(i).start()

        @pl.loop(first, owners)
        def _(i):
            o = owner_at(i)

            @pl.when(i > 0)
            def _():
                gz_from(o).wait_recv()

            for j in range(1, chips):
                gx(o, j).start()
            gc(o, x).start()

        @pl.loop(first, owners)
        def _(i):
            o = owner_at(i)
            for j in range(1, chips):
                gx_from(o, j).wait_recv()
                gc(o, chip_at(j)).start()

        @pl.loop(first, owners)
        def _(i):
            o = owner_at(i)
            for chip in range(chips):
                gc_from(o, chip).wait_recv()
                gc(o, chip).wait_send()
            for j in range(1, chips):
                gx(o, j).wait_send()

        for i in range(1, owners):
            gz(i).wait_send()

    def score(last):
        @pl.loop(0, owners)
        def _(o):
            held = cents[o].reshape(subs, width).astype(jnp.float32)
            squares[o] = jnp.sum(held * held, axis=1, keepdims=True)

        @pl.loop(0, blocks)
        def _(b):
            o = owner_ref[cluster_ref[b]]
            centre = cents[o].reshape(subs, width)
            dots = lax.dot_general(
                centre, rows[b], (((1,), (1,)), ((), ())), preferred_element_type=jnp.float32
            )
            logits = (2.0 * dots - squares[o]) * inv_root
            power = jnp.exp(logits - jnp.max(logits, axis=0, keepdims=True))
            weight = power / jnp.sum(power, axis=0, keepdims=True)
            wts[b] = weight.astype(jnp.bfloat16)
            if last:
                weight_out[b] = weight.T.astype(jnp.bfloat16)

    def rc(o):
        return remote(part.at[o, 1 - c], from_core.at[o], rc_send.at[o], rc_recv.at[o], "split", sibling)

    def rx(o, j):
        return remote(
            part.at[o, c, chip_at(j)], from_chip.at[o, j - 1], rx_send.at[o, j], rx_recv.at[o, j],
            "split", 2 * chip_at(j) + c,
        )

    def rx_from(o, j):
        return remote(
            part.at[o, c, x], from_chip.at[o, j - 1], rx_send.at[o, j], rx_recv.at[o, j],
            "split", 2 * chip_at(j) + c,
        )

    def rz(o):
        return remote(part.at[o, c, x], from_owner.at[z], rz_send.at[o], rz_recv.at[z], "dp", o)

    def rz_from(o):
        return remote(part.at[o, c, x], from_owner.at[o], rz_send.at[o], rz_recv.at[o], "dp", o)

    def weigh(o):
        ids = [jnp.int32(0)] * cap
        live = [jnp.int32(0)] * cap
        count = jnp.int32(0)
        for b in range(blocks):
            hit = jnp.where(owner_ref[cluster_ref[b]] == o, jnp.int32(1), jnp.int32(0))
            for j in range(cap):
                take = hit * jnp.where(count == j, jnp.int32(1), jnp.int32(0))
                ids[j] = ids[j] + take * b
                live[j] = live[j] + take
            count = count + hit
        mass = jnp.zeros((subs, 1), jnp.float32)
        for j in range(cap):
            piece = wts[ids[j]].astype(jnp.float32) * live[j].astype(jnp.float32)
            wcat[:, j * block_rows : (j + 1) * block_rows] = piece.astype(jnp.bfloat16)
            mass = mass + jnp.sum(piece, axis=1, keepdims=True)
        mass = split_mass(mass)
        step = 512 if width % 512 == 0 else width
        weights = wcat[...]
        for n in range(width // step):
            cols = slice(n * step, (n + 1) * step)
            taken = jnp.concatenate([rows[ids[j], :, cols] for j in range(cap)], axis=0)
            sums = jnp.dot(weights, taken, preferred_element_type=jnp.float32).astype(jnp.bfloat16)
            for q in range(parts):
                part[o, q % 2, q // 2, :, cols] = sums[q * portion : (q + 1) * portion]
        for q in range(parts):
            part[o, q % 2, q // 2, :, width:] = mass[q * portion : (q + 1) * portion]

    def store_sum(o, chip, total):
        part[o, c, chip, :, :width] = total[:, :width].astype(jnp.bfloat16)
        part[o, c, chip, :, width:] = split_mass(join_mass(total[:, width:]))

    def reduce(last):
        @pl.loop(0, owners + 2)
        def _(t):
            @pl.when(t < owners)
            def _():
                o = owner_at(1 + t)
                weigh(o)
                rc(o).start()

            @pl.when((t >= 1) & (t <= owners))
            def _():
                o = owner_at(t)
                rc(o).wait_recv()
                for j in range(1, chips + 1):
                    chip = chip_at(j)
                    store_sum(o, chip, part[o, c, chip].astype(jnp.float32) + from_core[o, chip].astype(jnp.float32))
                    if j < chips:
                        rx(o, j).start()

            @pl.when(t >= 2)
            def _():
                o = owner_at(t - 1)
                total = part[o, c, x].astype(jnp.float32)
                for j in range(1, chips):
                    rx_from(o, j).wait_recv()
                    total = total + from_chip[o, j - 1].astype(jnp.float32)
                store_sum(o, x, total)

                @pl.when(t < owners + 1)
                def _():
                    rz(o).start()

        total = part[z, c, x].astype(jnp.float32)
        for i in range(1, owners):
            o = owner_at(owners - i)
            rz_from(o).wait_recv()
            total = total + from_owner[o].astype(jnp.float32)
        mass = join_mass(total[:, width:])
        renewed = (total[:, :width] + PRIOR * cents[z, s].astype(jnp.float32)) / (mass + PRIOR)
        if last:
            centre_out[...] = renewed.astype(jnp.bfloat16)
        else:
            cents[z, s] = renewed.astype(jnp.bfloat16)

    def reduce_done():
        @pl.loop(0, owners)
        def _(t):
            o = owner_at(1 + t)
            rc(o).wait_send()
            for j in range(1, chips):
                rx(o, j).wait_send()

            @pl.when(t < owners - 1)
            def _():
                rz(o).wait_send()

    for sweep in range(ITERS):
        gather(1 if sweep == 0 else 0)
        if sweep == 0:
            load_rows.wait()
        else:
            reduce_done()
        score(sweep == ITERS - 1)
        reduce(sweep == ITERS - 1)
    reduce_done()


def body(embeddings, subcentroids, block_cluster, owner_map):
    owners = lax.axis_size("dp")
    parts = lax.axis_size("split")
    chips = parts // 2
    blocks = block_cluster.shape[0]
    total_rows, width = embeddings.shape
    block_rows = total_rows // blocks
    cap = max(2, 2 * blocks // owners)
    subs = subcentroids.shape[1]
    portion = subs // parts
    wide = width + LANES
    bf16 = jnp.bfloat16
    sems = pltpu.SemaphoreType.DMA
    flops = 2 * ITERS * subs * width * block_rows * (blocks + owners * cap)
    weights, centres = pl.pallas_call(
        functools.partial(kernel, owners, chips, cap),
        out_shape=(
            jax.ShapeDtypeStruct((blocks, block_rows, subs), bf16),
            jax.ShapeDtypeStruct((portion, width), bf16),
        ),
        in_specs=[
            pl.BlockSpec(memory_space=pltpu.SMEM),
            pl.BlockSpec(memory_space=pltpu.SMEM),
            pl.BlockSpec(memory_space=pl.ANY),
            pl.BlockSpec(memory_space=pl.ANY),
        ],
        out_specs=(
            pl.BlockSpec(memory_space=pltpu.VMEM),
            pl.BlockSpec(memory_space=pltpu.VMEM),
        ),
        scratch_shapes=[
            pltpu.VMEM((blocks, block_rows, width), bf16),
            pltpu.VMEM((owners, parts, portion, width), bf16),
            pltpu.VMEM((blocks, subs, block_rows), bf16),
            pltpu.VMEM((owners, subs, 1), jnp.float32),
            pltpu.VMEM((subs, cap * block_rows), bf16),
            pltpu.VMEM((owners, 2, chips, portion, wide), bf16),
            pltpu.VMEM((owners, chips, portion, wide), bf16),
            pltpu.VMEM((owners, max(1, chips - 1), portion, wide), bf16),
            pltpu.VMEM((owners, portion, wide), bf16),
            sems((2,)),
            sems((owners,)), sems((owners,)),
            sems((owners, chips)), sems((owners, chips)),
            sems((owners, chips)), sems((owners, chips)),
            sems((owners,)), sems((owners,)),
            sems((owners, chips)), sems((owners, chips)),
            sems((owners,)), sems((owners,)),
        ],
        compiler_params=pltpu.CompilerParams(
            collective_id=0, has_side_effects=True, vmem_limit_bytes=58 * 1024 * 1024
        ),
        cost_estimate=pl.CostEstimate(
            flops=flops, bytes_accessed=2 * total_rows * width, transcendentals=total_rows * subs
        ),
    )(
        block_cluster, owner_map,
        embeddings.reshape(blocks, block_rows, width),
        subcentroids.reshape(parts, portion, width),
    )
    return weights.reshape(total_rows, subs), centres[None]


def solution(mesh):
    return jax.shard_map(
        body,
        mesh=mesh,
        in_specs=(
            P(("groups", "dp", "split"), None),
            P(("groups", "dp"), None, None),
            P(("groups", "dp", "split")),
            P("groups"),
        ),
        out_specs=(P(("groups", "dp", "split"), None), P(("groups", "dp"), "split", None)),
        check_vma=False,
    )
```

time: 308 us -> 129 us (0.42)
  waiting for transfers between devices: 210 us -> 0 us
  Pallas kernels: 0 us -> 123 us
  matrix products: 21.3 us -> 0 us
  other arithmetic: 18.9 us -> 0 us
  starting transfers between devices: 16.2 us -> 0 us
  between operations: 14.1 us -> 0.64 us
  blocking collectives: 11.8 us -> 0 us
  local copies, waits for them, and re-layouts: 14.8 us -> 3.48 us
    all_to_all x3 -> x0, waiting for transfers between devices: 137 us -> none  [the longest x1 137 us: body(): lax.all_to_all(outgoing, 'dp', split_axis=0, concat_axis=0, tiled=True)]
    pallas_call x0 -> x1, Pallas kernels: none -> 123 us  [body(): pl.pallas_call(functools.partial(kernel, owners, chips, cap), out_shape=(...]
    psum x2 -> x0, waiting for transfers between devices: 73.7 us -> none  [body(): summed, mass_all = lax.psum((weighted, weight_mass), 'split')]
    dot_general x4 -> x0, matrix products: 21.3 us -> none  [the longest x2 11.9 us: body(): lax.dot_general(masked, flat_rows, (((0,), (0,)), ((), ())), preferred_el...]
    all_to_all x3 -> x0, starting transfers between devices: 16.2 us -> none  [the longest x1 6.32 us: body(): lax.all_to_all(flags, 'dp', split_axis=0, concat_axis=0, tiled=True)]
    psum x2 -> x0, blocking collectives: 11.8 us -> none  [body(): summed, mass_all = lax.psum((weighted, weight_mass), 'split')]
    select_n x4 -> x0, other arithmetic: 8.24 us -> none  [the longest x1 6.19 us: body(): jnp.where(occupied[:, None, None], jnp.take(blocks, source_block, axis=0)...]
    gather x2 -> x0, local copies, waits for them, and re-layouts: 6.23 us -> none  [the longest x1 3.61 us: body(): jnp.take(blocks, source_block, axis=0)]
  transfers between devices with their start and end apart: 5 -> 0, of which waited for: 3 -> 0; matrix products, arithmetic and copies ran while one was open for 6% -> 0% of each run, Pallas kernels for 0% -> 0%
where the time goes in v1:
time: 129 us; the launch traced here: 127 us
  Pallas kernels  123 us (95%)
  local copies, waits for them, and re-layouts  3.48 us (3%)
    pallas_call x1, Pallas kernels, body(): pl.pallas_call(functools.partial(kernel, owners, chips, cap), out_shape=(...  123 us
    unnamed x2, local copies, waits for them, and re-layouts  3.48 us

profile of v1, /device:TPU:0, one launch (start us, length us, event | category | flops | bytes accessed | tf_op | source)
XLA Modules:
  0.0 127.1 jit_solution(10219566178360098255)
XLA Ops:
  0.6 123.0 %shard_map.59 = (bf16[8,128,256]{2,1,0:T(8,128)(2,1)}, bf16[64,1536]{1,0:T(8,128)(2,1)}) custom-call(s32[8]{0:T(128)} %cluster_ref.1, s32[4]{0:T(128)} %owner_ref.1, bf16[8,128,1536]{2,1,0:T(8,128)(2,1)} %bitcast.6, bf16[4,64,1536]{2,1,0:T(8,128)(2,1)} %bitcast.7), custom_call_target="tpu_custom_call" | custom-call | flops 4831838208 | bytes 3145728 | tf_op jit(solution)/shard_map/pallas_call | solution.py:283
  123.6 1.9 %copy.8 = bf16[1024,256]{1,0:T(8,128)(2,1)} copy(bf16[1024,256]{1,0:T(8,128)(2,1)} %bitcast.4) | data formatting | bytes 1048576
  125.5 1.6 %copy.9 = bf16[1,64,1536]{2,1,0:T(8,128)(2,1)} copy(bf16[1,64,1536]{2,1,0:T(8,128)(2,1)} %bitcast.5) | data formatting | bytes 393216

commit v2 on v1

v2 whole, which is shorter than its diff:
```python
import functools

import jax
import jax.numpy as jnp
from jax import lax
from jax.experimental import pallas as pl
from jax.experimental.pallas import tpu as pltpu
from jax.sharding import PartitionSpec as P

MESH = pl.DeviceIdType.MESH
ITERS = 2
PRIOR = 4.0
LANES = 128
LAG = 4


def split_mass(mass):
    high = mass.astype(jnp.bfloat16).astype(jnp.float32)
    lane = lax.broadcasted_iota(jnp.int32, (mass.shape[0], LANES), 1)
    return jnp.where(lane < LANES // 2, high, mass - high).astype(jnp.bfloat16)


def join_mass(pair):
    return pair[:, :1] + pair[:, LANES // 2 : LANES // 2 + 1]


def kernel(
    owners, chips, cap,
    cluster_ref, owner_ref, rows_hbm, sub_hbm,
    weight_out, centre_out,
    rows, cents, wts, squares, wcat, part, from_core, from_chip, from_owner, sums,
    load_sem, gz_send, gz_recv, gx_send, gx_recv, gc_send, gc_recv,
    rc_send, rc_recv, rx_send, rx_recv, rz_send, rz_recv,
):
    blocks, block_rows, width = rows.shape
    parts, portion = cents.shape[1], cents.shape[2]
    subs = parts * portion
    inv_root = width ** (-0.5)
    z = lax.axis_index("dp")
    s = lax.axis_index("split")
    x = lax.div(s, 2)
    c = s - 2 * x
    sibling = 2 * x + (1 - c)
    halves = 2 if portion % 32 == 0 else 1
    rows_half = portion // halves

    def span(h):
        return pl.ds(pl.multiple_of(h * rows_half, rows_half), rows_half)

    def chip_at(j):
        return lax.rem(x + j, chips)

    def remote(src, dst, send, recv, axis, index):
        return pltpu.make_async_remote_copy(
            src_ref=src, dst_ref=dst, send_sem=send, recv_sem=recv,
            device_id={axis: index}, device_id_type=MESH,
        )

    load_rows = pltpu.make_async_copy(rows_hbm, rows, load_sem.at[0])
    load_sub = pltpu.make_async_copy(sub_hbm, cents.at[z], load_sem.at[1])
    load_sub.start()
    load_rows.start()

    barrier = pltpu.get_barrier_semaphore()
    pl.semaphore_signal(barrier, inc=1, device_id={"split": sibling}, device_id_type=MESH)
    for j in range(1, chips):
        pl.semaphore_signal(barrier, inc=1, device_id={"split": 2 * chip_at(j) + c}, device_id_type=MESH)
    for way in range(2):

        @pl.when(z < owners - 1 if way == 0 else z > 0)
        def _():
            pl.semaphore_signal(barrier, inc=1, device_id={"dp": z + 1 - 2 * way}, device_id_type=MESH)

    links = jnp.where(z > 0, 1, 0) + jnp.where(z < owners - 1, 1, 0)
    pl.semaphore_wait(barrier, chips + links)
    load_sub.wait()

    def gz(o, h, way):
        ref = cents.at[o, s, span(h)]
        return remote(ref, ref, gz_send.at[o, h, way], gz_recv.at[o, h], "dp", z + 1 - 2 * way)

    def gz_from(o, h, way):
        ref = cents.at[o, s, span(h)]
        return remote(ref, ref, gz_send.at[o, h, way], gz_recv.at[o, h], "dp", z - 1 + 2 * way)

    def has_next(way):
        return z < owners - 1 if way == 0 else z > 0

    def gx(o, h, j):
        ref = cents.at[o, s, span(h)]
        return remote(ref, ref, gx_send.at[o, h, j], gx_recv.at[o, h, x], "split", 2 * chip_at(j) + c)

    def gx_from(o, h, j):
        ref = cents.at[o, 2 * chip_at(j) + c, span(h)]
        return remote(ref, ref, gx_send.at[o, h, j], gx_recv.at[o, h, chip_at(j)], "split", 2 * chip_at(j) + c)

    def gc(o, h, chip):
        ref = cents.at[o, 2 * chip + c, span(h)]
        return remote(ref, ref, gc_send.at[o, h, chip], gc_recv.at[o, h, chip], "split", sibling)

    def gc_from(o, h, chip):
        ref = cents.at[o, 2 * chip + 1 - c, span(h)]
        return remote(ref, ref, gc_send.at[o, h, chip], gc_recv.at[o, h, chip], "split", sibling)

    def spread(o, h):
        for j in range(1, chips):
            gx(o, h, j).start()
        gc(o, h, x).start()

    def pass_on(o, h):
        for j in range(1, chips):
            gx_from(o, h, j).wait_recv()
            gc(o, h, chip_at(j)).start()

    def settle(o):
        for h in range(halves):
            for chip in range(chips):
                gc_from(o, h, chip).wait_recv()
                gc(o, h, chip).wait_send()
            for j in range(1, chips):
                gx(o, h, j).wait_send()

    def at_distance(k, act):
        for way in range(2):
            o = z - k if way == 0 else z + k

            @pl.when(o >= 0 if way == 0 else o < owners)
            def _():
                act(o, way)

    def onward(o, h, way, done):
        @pl.when(has_next(way))
        def _():
            if done:
                gz(o, h, way).wait_send()
            else:
                gz(o, h, way).start()

    def gather(first):
        for h in range(halves):
            for way in range(2):
                onward(z, h, way, False)
            if not first:
                spread(z, h)

        @pl.loop(1, owners + 1)
        def _(k):
            for h in range(halves):

                def arrive(o, way, h=h):
                    gz_from(o, h, way).wait_recv()
                    onward(o, h, way, False)
                    spread(o, h)

                at_distance(k, arrive)

                @pl.when(k > 1)
                def _():
                    at_distance(k - 1, lambda o, way, h=h: pass_on(o, h))

                if not first:

                    @pl.when(k == 1)
                    def _():
                        pass_on(z, h)

        def finish(o, way):
            for h in range(halves):
                onward(o, h, way, True)
            settle(o)

        for h in range(halves):
            for way in range(2):
                onward(z, h, way, True)
        if not first:
            settle(z)

        @pl.loop(1, owners)
        def _(k):
            at_distance(k, finish)

    def score(last):
        @pl.loop(0, owners)
        def _(o):
            held = cents[o].reshape(subs, width).astype(jnp.float32)
            squares[o] = jnp.sum(held * held, axis=1, keepdims=True)

        @pl.loop(0, blocks)
        def _(b):
            o = owner_ref[cluster_ref[b]]
            centre = cents[o].reshape(subs, width)
            dots = lax.dot_general(
                centre, rows[b], (((1,), (1,)), ((), ())), preferred_element_type=jnp.float32
            )
            logits = (2.0 * dots - squares[o]) * inv_root
            power = jnp.exp(logits - jnp.max(logits, axis=0, keepdims=True))
            weight = power / jnp.sum(power, axis=0, keepdims=True)
            wts[b] = weight.astype(jnp.bfloat16)
            if last:
                weight_out[b] = weight.T.astype(jnp.bfloat16)

    def rc(o):
        return remote(part.at[o, 1 - c], from_core.at[o], rc_send.at[o], rc_recv.at[o], "split", sibling)

    def rx(o, h, j):
        return remote(
            part.at[o, c, chip_at(j), span(h)], from_chip.at[o, j - 1, span(h)],
            rx_send.at[o, h, j], rx_recv.at[o, h, j], "split", 2 * chip_at(j) + c,
        )

    def rz(o, h, way):
        slot = o if way == 0 else jnp.where(o == z - 1, owners, o)
        return remote(
            part.at[o, c, x, span(h)], from_owner.at[slot, span(h)],
            rz_send.at[o, h], rz_recv.at[slot, h], "dp", z + 1 - 2 * way,
        )

    def rz_from(o, h, way):
        slot = o if way == 0 else jnp.where(o == z, owners, o)
        return slot, remote(
            part.at[o, c, x, span(h)], from_owner.at[slot, span(h)],
            rz_send.at[o, h], rz_recv.at[slot, h], "dp", z - 1 + 2 * way,
        )

    below, above = z, owners - 1 - z
    far = jnp.maximum(below, above)
    near = jnp.minimum(below, above)
    far_sign = jnp.where(above >= below, 1, -1)

    def farthest(t):
        u = t - (far - near)
        half = lax.div(jnp.maximum(u, 0), 2)
        sign = jnp.where(u - 2 * half == 1, -far_sign, far_sign)
        return jnp.where(u < 0, z + far_sign * (far - t), z + sign * (near - half))

    def weigh(o):
        ids = [jnp.int32(0)] * cap
        live = [jnp.int32(0)] * cap
        count = jnp.int32(0)
        for b in range(blocks):
            hit = jnp.where(owner_ref[cluster_ref[b]] == o, jnp.int32(1), jnp.int32(0))
            for j in range(cap):
                take = hit * jnp.where(count == j, jnp.int32(1), jnp.int32(0))
                ids[j] = ids[j] + take * b
                live[j] = live[j] + take
            count = count + hit
        mass = jnp.zeros((subs, 1), jnp.float32)
        for j in range(cap):
            piece = wts[ids[j]].astype(jnp.float32) * live[j].astype(jnp.float32)
            wcat[:, j * block_rows : (j + 1) * block_rows] = piece.astype(jnp.bfloat16)
            mass = mass + jnp.sum(piece, axis=1, keepdims=True)
        mass = split_mass(mass)
        step = 512 if width % 512 == 0 else width
        weights = wcat[...]
        for n in range(width // step):
            cols = slice(n * step, (n + 1) * step)
            taken = jnp.concatenate([rows[ids[j], :, cols] for j in range(cap)], axis=0)
            product = jnp.dot(weights, taken, preferred_element_type=jnp.float32).astype(jnp.bfloat16)
            for q in range(parts):
                part[o, q % 2, q // 2, :, cols] = product[q * portion : (q + 1) * portion]
        for q in range(parts):
            part[o, q % 2, q // 2, :, width:] = mass[q * portion : (q + 1) * portion]

    def store_sum(o, chip, h, total):
        part[o, c, chip, span(h), :width] = total[:, :width].astype(jnp.bfloat16)
        part[o, c, chip, span(h), width:] = split_mass(join_mass(total[:, width:]))

    def over_chips(o, h):
        total = part[o, c, x, span(h)].astype(jnp.float32)
        for j in range(1, chips):
            rx(o, h, chips - j).wait_recv()
            total = total + from_chip[o, chips - j - 1, span(h)].astype(jnp.float32)
        return total

    def reduce(last):
        units = owners * halves

        def unit(u):
            t = lax.div(u, halves)
            return farthest(t), u - t * halves

        @pl.loop(0, units + 1)
        def _(u):
            o, h = unit(u)

            @pl.when((u < units) & (h == 0))
            def _():
                weigh(o)
                rc(o).start()

            before, hb = unit(jnp.maximum(u - 1, 0))

            @pl.when(u >= 1)
            def _():
                @pl.when(hb == 0)
                def _():
                    rc(before).wait_recv()

                for j in range(1, chips + 1):
                    chip = chip_at(j)
                    store_sum(
                        before, chip, hb,
                        part[before, c, chip, span(hb)].astype(jnp.float32)
                        + from_core[before, chip, span(hb)].astype(jnp.float32),
                    )
                    if j < chips:
                        rx(before, hb, j).start()

            @pl.when(u >= LAG)
            def _():
                forward(*unit(jnp.maximum(u - LAG, 0)))

        for u in range(units + 1 - LAG, units):
            forward(*unit(u))
        for h in range(halves):
            sums[...] = over_chips(z, h)
            for way in range(2):

                @pl.when(z > 0 if way == 0 else z < owners - 1)
                def _():
                    slot, copy = rz_from(z, h, way)
                    copy.wait_recv()
                    sums[...] += from_owner[slot, span(h)].astype(jnp.float32)

            mass = join_mass(sums[:, width:])
            renewed = (sums[:, :width] + PRIOR * cents[z, s, span(h)].astype(jnp.float32)) / (mass + PRIOR)
            if last:
                centre_out[span(h)] = renewed.astype(jnp.bfloat16)
            else:
                cents[z, s, span(h)] = renewed.astype(jnp.bfloat16)

    def forward(o, h):
        for way in range(2):

            @pl.when(o > z if way == 0 else o < z)
            def _():
                total = over_chips(o, h)
                store_sum(o, x, h, total)

                @pl.when(z > 0 if way == 0 else z < owners - 1)
                def _():
                    slot, copy = rz_from(o, h, way)
                    copy.wait_recv()
                    store_sum(o, x, h, total + from_owner[slot, span(h)].astype(jnp.float32))

                rz(o, h, way).start()

    def reduce_done():
        @pl.loop(0, owners)
        def _(o):
            rc(o).wait_send()
            for h in range(halves):
                for j in range(1, chips):
                    rx(o, h, j).wait_send()

                @pl.when(o > z)
                def _():
                    rz(o, h, 0).wait_send()

                @pl.when(o < z)
                def _():
                    rz(o, h, 1).wait_send()

    for sweep in range(ITERS):
        gather(sweep == 0)
        if sweep == 0:
            load_rows.wait()
        else:
            reduce_done()
        score(sweep == ITERS - 1)
        reduce(sweep == ITERS - 1)
    reduce_done()


def body(embeddings, subcentroids, block_cluster, owner_map):
    owners = lax.axis_size("dp")
    parts = lax.axis_size("split")
    chips = parts // 2
    blocks = block_cluster.shape[0]
    total_rows, width = embeddings.shape
    block_rows = total_rows // blocks
    cap = max(2, 2 * blocks // owners)
    subs = subcentroids.shape[1]
    portion = subs // parts
    wide = width + LANES
    bf16 = jnp.bfloat16
    sems = pltpu.SemaphoreType.DMA
    flops = 2 * ITERS * subs * width * block_rows * (blocks + owners * cap)
    weights, centres = pl.pallas_call(
        functools.partial(kernel, owners, chips, cap),
        out_shape=(
            jax.ShapeDtypeStruct((blocks, block_rows, subs), bf16),
            jax.ShapeDtypeStruct((portion, width), bf16),
        ),
        in_specs=[
            pl.BlockSpec(memory_space=pltpu.SMEM),
            pl.BlockSpec(memory_space=pltpu.SMEM),
            pl.BlockSpec(memory_space=pl.ANY),
            pl.BlockSpec(memory_space=pl.ANY),
        ],
        out_specs=(
            pl.BlockSpec(memory_space=pltpu.VMEM),
            pl.BlockSpec(memory_space=pltpu.VMEM),
        ),
        scratch_shapes=[
            pltpu.VMEM((blocks, block_rows, width), bf16),
            pltpu.VMEM((owners, parts, portion, width), bf16),
            pltpu.VMEM((blocks, subs, block_rows), bf16),
            pltpu.VMEM((owners, subs, 1), jnp.float32),
            pltpu.VMEM((subs, cap * block_rows), bf16),
            pltpu.VMEM((owners, 2, chips, portion, wide), bf16),
            pltpu.VMEM((owners, chips, portion, wide), bf16),
            pltpu.VMEM((owners, max(1, chips - 1), portion, wide), bf16),
            pltpu.VMEM((owners + 1, portion, wide), bf16),
            pltpu.VMEM((portion // (2 if portion % 32 == 0 else 1), wide), jnp.float32),
            sems((2,)),
            sems((owners, 2, 2)), sems((owners, 2)),
            sems((owners, 2, chips)), sems((owners, 2, chips)),
            sems((owners, 2, chips)), sems((owners, 2, chips)),
            sems((owners,)), sems((owners,)),
            sems((owners, 2, chips)), sems((owners, 2, chips)),
            sems((owners, 2)), sems((owners + 1, 2)),
        ],
        compiler_params=pltpu.CompilerParams(
            collective_id=0, has_side_effects=True, vmem_limit_bytes=58 * 1024 * 1024
        ),
        cost_estimate=pl.CostEstimate(
            flops=flops, bytes_accessed=2 * total_rows * width, transcendentals=total_rows * subs
        ),
    )(
        block_cluster, owner_map,
        embeddings.reshape(blocks, block_rows, width),
        subcentroids.reshape(parts, portion, width),
    )
    return weights.reshape(total_rows, subs), centres[None]


def solution(mesh):
    return jax.shard_map(
        body,
        mesh=mesh,
        in_specs=(
            P(("groups", "dp", "split"), None),
            P(("groups", "dp"), None, None),
            P(("groups", "dp", "split")),
            P("groups"),
        ),
        out_specs=(P(("groups", "dp", "split"), None), P(("groups", "dp"), "split", None)),
        check_vma=False,
    )
```

time: 129 us -> 108 us (0.84); the launches traced: 127 us -> 108 us
  Pallas kernels: 123 us -> 104 us
    pallas_call x1, Pallas kernels: 123 us -> 104 us  [body(): pl.pallas_call(functools.partial(kernel, owners, chips, cap), out_shape=(...]
where the time goes in v2:
time: 108 us
  Pallas kernels  104 us (96%)
  local copies, waits for them, and re-layouts  3.48 us (3%)
    pallas_call x1, Pallas kernels, body(): pl.pallas_call(functools.partial(kernel, owners, chips, cap), out_shape=(...  104 us
    unnamed x2, local copies, waits for them, and re-layouts  3.48 us

profile of v2, /device:TPU:0, one launch (start us, length us, event | category | flops | bytes accessed | tf_op | source)
XLA Modules:
  0.0 107.6 jit_solution(10426087669625869886)
XLA Ops:
  0.6 103.5 %shard_map.59 = (bf16[8,128,256]{2,1,0:T(8,128)(2,1)}, bf16[64,1536]{1,0:T(8,128)(2,1)}) custom-call(s32[8]{0:T(128)} %cluster_ref.1, s32[4]{0:T(128)} %owner_ref.1, bf16[8,128,1536]{2,1,0:T(8,128)(2,1)} %bitcast.6, bf16[4,64,1536]{2,1,0:T(8,128)(2,1)} %bitcast.7), custom_call_target="tpu_custom_call" | custom-call | flops 4831838208 | bytes 3145728 | tf_op jit(solution)/shard_map/pallas_call | solution.py:389
  104.2 1.9 %copy.8 = bf16[1024,256]{1,0:T(8,128)(2,1)} copy(bf16[1024,256]{1,0:T(8,128)(2,1)} %bitcast.4) | data formatting | bytes 1048576
  106.0 1.6 %copy.9 = bf16[1,64,1536]{2,1,0:T(8,128)(2,1)} copy(bf16[1,64,1536]{2,1,0:T(8,128)(2,1)} %bitcast.5) | data formatting | bytes 393216

commit v3 on v2

--- a/solution.py
+++ b/solution.py
@@ -28,7 +28,7 @@
     owners, chips, cap,
     cluster_ref, owner_ref, rows_hbm, sub_hbm,
     weight_out, centre_out,
-    rows, cents, wts, squares, wcat, part, from_core, from_chip, from_owner, sums,
+    rows, cents, wts, wcat, part, from_core, from_chip, from_owner, sums,
     load_sem, gz_send, gz_recv, gx_send, gx_recv, gc_send, gc_recv,
     rc_send, rc_recv, rx_send, rx_recv, rz_send, rz_recv,
 ):
@@ -179,26 +179,6 @@
         def _(k):
             at_distance(k, finish)
 
-    def score(last):
-        @pl.loop(0, owners)
-        def _(o):
-            held = cents[o].reshape(subs, width).astype(jnp.float32)
-            squares[o] = jnp.sum(held * held, axis=1, keepdims=True)
-
-        @pl.loop(0, blocks)
-        def _(b):
-            o = owner_ref[cluster_ref[b]]
-            centre = cents[o].reshape(subs, width)
-            dots = lax.dot_general(
-                centre, rows[b], (((1,), (1,)), ((), ())), preferred_element_type=jnp.float32
-            )
-            logits = (2.0 * dots - squares[o]) * inv_root
-            power = jnp.exp(logits - jnp.max(logits, axis=0, keepdims=True))
-            weight = power / jnp.sum(power, axis=0, keepdims=True)
-            wts[b] = weight.astype(jnp.bfloat16)
-            if last:
-                weight_out[b] = weight.T.astype(jnp.bfloat16)
-
     def rc(o):
         return remote(part.at[o, 1 - c], from_core.at[o], rc_send.at[o], rc_recv.at[o], "split", sibling)
 
@@ -233,7 +213,7 @@
         sign = jnp.where(u - 2 * half == 1, -far_sign, far_sign)
         return jnp.where(u < 0, z + far_sign * (far - t), z + sign * (near - half))
 
-    def weigh(o):
+    def weigh(o, last):
         ids = [jnp.int32(0)] * cap
         live = [jnp.int32(0)] * cap
         count = jnp.int32(0)
@@ -244,9 +224,20 @@
                 ids[j] = ids[j] + take * b
                 live[j] = live[j] + take
             count = count + hit
+        centre = cents[o].reshape(subs, width)
+        held = centre.astype(jnp.float32)
+        squares = jnp.sum(held * held, axis=1, keepdims=True)
         mass = jnp.zeros((subs, 1), jnp.float32)
         for j in range(cap):
-            piece = wts[ids[j]].astype(jnp.float32) * live[j].astype(jnp.float32)
+            dots = lax.dot_general(
+                centre, rows[ids[j]], (((1,), (1,)), ((), ())), preferred_element_type=jnp.float32
+            )
+            logits = (2.0 * dots - squares) * inv_root
+            power = jnp.exp(logits - jnp.max(logits, axis=0, keepdims=True))
+            weight = (power / jnp.sum(power, axis=0, keepdims=True)).astype(jnp.bfloat16)
+            if last:
+                wts[o * cap + j] = weight
+            piece = weight.astype(jnp.float32) * live[j].astype(jnp.float32)
             wcat[:, j * block_rows : (j + 1) * block_rows] = piece.astype(jnp.bfloat16)
             mass = mass + jnp.sum(piece, axis=1, keepdims=True)
         mass = split_mass(mass)
@@ -285,7 +276,7 @@
 
             @pl.when((u < units) & (h == 0))
             def _():
-                weigh(o)
+                weigh(o, last)
                 rc(o).start()
 
             before, hb = unit(jnp.maximum(u - 1, 0))
@@ -310,6 +301,8 @@
             def _():
                 forward(*unit(jnp.maximum(u - LAG, 0)))
 
+        if last:
+            bring_home()
         for u in range(units + 1 - LAG, units):
             forward(*unit(u))
         for h in range(halves):
@@ -328,6 +321,14 @@
                 centre_out[span(h)] = renewed.astype(jnp.bfloat16)
             else:
                 cents[z, s, span(h)] = renewed.astype(jnp.bfloat16)
+
+    def bring_home():
+        for b in range(blocks):
+            o = owner_ref[cluster_ref[b]]
+            rank = jnp.int32(0)
+            for e in range(b):
+                rank = rank + jnp.where(owner_ref[cluster_ref[e]] == o, jnp.int32(1), jnp.int32(0))
+            weight_out[b] = wts[o * cap + rank].astype(jnp.float32).T.astype(jnp.bfloat16)
 
     def forward(o, h):
         for way in range(2):
@@ -367,7 +368,6 @@
             load_rows.wait()
         else:
             reduce_done()
-        score(sweep == ITERS - 1)
         reduce(sweep == ITERS - 1)
     reduce_done()
 
@@ -405,8 +405,7 @@
         scratch_shapes=[
             pltpu.VMEM((blocks, block_rows, width), bf16),
             pltpu.VMEM((owners, parts, portion, width), bf16),
-            pltpu.VMEM((blocks, subs, block_rows), bf16),
-            pltpu.VMEM((owners, subs, 1), jnp.float32),
+            pltpu.VMEM((owners * cap, subs, block_rows), bf16),
             pltpu.VMEM((subs, cap * block_rows), bf16),
             pltpu.VMEM((owners, 2, chips, portion, wide), bf16),
             pltpu.VMEM((owners, chips, portion, wide), bf16),

time: 108 us -> 105 us (0.972)
  Pallas kernels: 104 us -> 101 us
    pallas_call x1, Pallas kernels: 104 us -> 101 us  [body(): pl.pallas_call(functools.partial(kernel, owners, chips, cap), out_shape=(...]
where the time goes in v3:
time: 105 us
  Pallas kernels  101 us (96%)
  local copies, waits for them, and re-layouts  3.48 us (3%)
    pallas_call x1, Pallas kernels, body(): pl.pallas_call(functools.partial(kernel, owners, chips, cap), out_shape=(...  101 us
    unnamed x2, local copies, waits for them, and re-layouts  3.48 us

profile of v3, /device:TPU:0, one launch (start us, length us, event | category | flops | bytes accessed | tf_op | source)
XLA Modules:
  0.0 104.8 jit_solution(15121700768157191090)
XLA Ops:
  0.6 100.7 %shard_map.59 = (bf16[8,128,256]{2,1,0:T(8,128)(2,1)}, bf16[64,1536]{1,0:T(8,128)(2,1)}) custom-call(s32[8]{0:T(128)} %cluster_ref.1, s32[4]{0:T(128)} %owner_ref.1, bf16[8,128,1536]{2,1,0:T(8,128)(2,1)} %bitcast.6, bf16[4,64,1536]{2,1,0:T(8,128)(2,1)} %bitcast.7), custom_call_target="tpu_custom_call" | custom-call | flops 4831838208 | bytes 3145728 | tf_op jit(solution)/shard_map/pallas_call | solution.py:389
  101.4 1.9 %copy.8 = bf16[1024,256]{1,0:T(8,128)(2,1)} copy(bf16[1024,256]{1,0:T(8,128)(2,1)} %bitcast.4) | data formatting | bytes 1048576
  103.2 1.6 %copy.9 = bf16[1,64,1536]{2,1,0:T(8,128)(2,1)} copy(bf16[1,64,1536]{2,1,0:T(8,128)(2,1)} %bitcast.5) | data formatting | bytes 393216

commit v4 on v3

--- a/solution.py
+++ b/solution.py
@@ -137,11 +137,10 @@
                 gz(o, h, way).start()
 
     def gather(first):
-        for h in range(halves):
-            for way in range(2):
-                onward(z, h, way, False)
-            if not first:
-                spread(z, h)
+        if first:
+            for h in range(halves):
+                for way in range(2):
+                    onward(z, h, way, False)
 
         @pl.loop(1, owners + 1)
         def _(k):
@@ -321,6 +320,9 @@
                 centre_out[span(h)] = renewed.astype(jnp.bfloat16)
             else:
                 cents[z, s, span(h)] = renewed.astype(jnp.bfloat16)
+                for way in range(2):
+                    onward(z, h, way, False)
+                spread(z, h)
 
     def bring_home():
         for b in range(blocks):

time: 105 us -> 104 us (level)
  Pallas kernels: 101 us -> 99.6 us
    pallas_call x1, Pallas kernels: 101 us -> 99.6 us  [body(): pl.pallas_call(functools.partial(kernel, owners, chips, cap), out_shape=(...]
where the time goes in v4:
time: 104 us
  Pallas kernels  99.6 us (96%)
  local copies, waits for them, and re-layouts  3.48 us (3%)
    pallas_call x1, Pallas kernels, body(): pl.pallas_call(functools.partial(kernel, owners, chips, cap), out_shape=(...  99.6 us
    unnamed x2, local copies, waits for them, and re-layouts  3.48 us

profile of v4, /device:TPU:0, one launch (start us, length us, event | category | flops | bytes accessed | tf_op | source)
XLA Modules:
  0.0 103.8 jit_solution(2063508490565279133)
XLA Ops:
  0.6 99.6 %shard_map.59 = (bf16[8,128,256]{2,1,0:T(8,128)(2,1)}, bf16[64,1536]{1,0:T(8,128)(2,1)}) custom-call(s32[8]{0:T(128)} %cluster_ref.1, s32[4]{0:T(128)} %owner_ref.1, bf16[8,128,1536]{2,1,0:T(8,128)(2,1)} %bitcast.6, bf16[4,64,1536]{2,1,0:T(8,128)(2,1)} %bitcast.7), custom_call_target="tpu_custom_call" | custom-call | flops 4831838208 | bytes 3145728 | tf_op jit(solution)/shard_map/pallas_call | solution.py:391
  100.3 1.9 %copy.8 = bf16[1024,256]{1,0:T(8,128)(2,1)} copy(bf16[1024,256]{1,0:T(8,128)(2,1)} %bitcast.4) | data formatting | bytes 1048576
  102.2 1.6 %copy.9 = bf16[1,64,1536]{2,1,0:T(8,128)(2,1)} copy(bf16[1,64,1536]{2,1,0:T(8,128)(2,1)} %bitcast.5) | data formatting | bytes 393216
